TPU v7x, 32 devices: a whole 2x2x4 slice. The times are simulated.
32 devices in a mesh: groups: 2 (over y), aux: 4 (over z), atoms: 4 (over x, core).
Axes of the slice: x: 2, y: 2, z: 4, core: 2. Of those that a mesh axis runs over, the one named last changes fastest.
Arguments:
- three_center: bfloat16 [2048, 4, 3, 128], P('atoms', 'aux'), may hold values from -0.3125 to 0.3125
- virt_density: bfloat16 [4096, 2048], P(('groups', 'atoms')), parts along dimension 0, may hold values from -6 to 6
- occ_density: bfloat16 [4096, 2048], P('groups', 'atoms'), parts along dimension 0, as said below
- partner_list: int32 [16, 3], replicated, may hold values from 0 to 15, as said below
- partner_count: int32 [16], replicated, may hold values from 1 to 3, 30 in all
Outputs:
- polarizability: float32 [8, 4], P(('groups', 'aux'), 'atoms'), parts along dimension 0
There are 2 independent parts, one for each index of `groups`. A program takes and returns all parts, laid end to end along the dimension named above; an argument that names none is the same for every part. Nothing has to cross between parts.
Inputs may be any that keep to these rules, and one draw needn't show every extreme that they name: occ_density is symmetric. `partner_list`: each row lists 3 different blocks, the first being the row's own block.
All inputs are finite; a program needn't handle non-finite values.
Results may differ from a plain program's by a relative error of at most 0.005.
Values may be sent and summed in bfloat16 or wider, within the bound.
No kernel may reach another device: no remote copies, remote signals or barrier semaphores. Data moves between devices by JAX's collectives and lax.ppermute only.
A program may use at most 64 MiB of HBM per device.

v0:
```python
import functools

import jax
import jax.numpy as jnp
from jax import lax
from jax.experimental import pallas as pl
from jax.experimental.pallas import tpu as pltpu
from jax.sharding import PartitionSpec as P

BS = 128
KN = 3
MIB = 1 << 20


def swap(x, axes, sizes, move):
    perm = []
    total = 1
    for size in sizes:
        total *= size
    for source in range(total):
        coords, rest = [], source
        for size in reversed(sizes):
            coords.append(rest % size)
            rest //= size
        target = 0
        for size, at in zip(sizes, move(*reversed(coords))):
            target = target * size + at
        perm.append((source, target))
    return lax.ppermute(x, axes, perm)


def select(n_blocks, where, virt_ref, out_ref, buf, sem):
    def copy(i):
        columns = pl.ds(pl.multiple_of((2 * i + where[1]) * BS, BS), BS)
        return pltpu.make_async_copy(virt_ref.at[:, columns], buf.at[i], sem.at[i])

    for i in range(n_blocks):
        copy(i).start()
    for i in range(n_blocks):
        copy(i).wait()
        out_ref[i * BS : (i + 1) * BS, :] = buf[i].T


def after(x, *others):
    return lax.optimization_barrier((x,) + others)[0]


def contract(n_centers, where, plist, pcount, *refs):
    v_refs, m_refs, occ_ref, c_refs = refs[0:4], refs[4:12], refs[12], refs[13 : 13 + n_centers]
    out_ref, prod, acc, listed, place = refs[13 + n_centers :]
    own, parity, plane, aux_at = where[0], where[1], where[2], where[3]
    n_q = acc.shape[1]
    rows = v_refs[0].shape[1]
    blocks_here = rows // BS
    n_places = prod.shape[0]

    def used(b, k):
        block = own * blocks_here + b
        return (k < pcount[block]) & ((plist[k, block] & 1) == parity)

    def column(b, k):
        return plist[k, own * blocks_here + b] >> 1

    for c in range(n_places):
        place[c] = -1
    count = jnp.int32(blocks_here // 2)
    for i in range(blocks_here // 2):
        c = own * (blocks_here // 2) + i
        place[c] = i
        listed[i] = c
    for k in range(1, KN):
        for b in range(blocks_here):
            c = column(b, k)
            new = used(b, k) & (place[c] < 0)

            @pl.when(new)
            def _(c=c, count=count):
                place[c] = count
                listed[count] = c

            count = count + new.astype(jnp.int32)

    @pl.when((count & 1) == 1)
    def _():
        listed[count] = listed[count - 1]

    acc[...] = jnp.zeros_like(acc)

    def one_group(g, carry):
        spans = [pl.ds(pl.multiple_of(listed[2 * g + h] * BS, BS), BS) for h in range(2)]
        for i in range(4):
            for j in range(blocks_here):
                block = (own ^ i) * blocks_here + j
                span = slice(j * BS, (j + 1) * BS)
                parts = [jnp.concatenate([v_refs[i][r, span] for r in spans], axis=0)]
                weights = [jnp.concatenate([m_refs[4 * s + i][0, span, :] for s in range(2)])]
                for k in range(1, KN):
                    p = plist[k, block]
                    shard = (p // blocks_here) ^ own
                    at = pl.ds(pl.multiple_of(lax.rem(p, blocks_here) * BS, BS), BS)
                    part = jnp.concatenate([v_refs[0][r, at] for r in spans], axis=0)
                    for q in range(1, 4):
                        other = jnp.concatenate([v_refs[q][r, at] for r in spans], axis=0)
                        part = jnp.where(shard == q, other, part)
                    parts.append(part)
                    weight = jnp.concatenate([m_refs[4 * s + i][k, span, :] for s in range(2)])
                    weights.append(jnp.where(k < pcount[block], weight, jnp.zeros_like(weight)))
                res = lax.dot_general(
                    jnp.concatenate(parts, axis=1),
                    jnp.concatenate(weights, axis=1),
                    (((1,), (1,)), ((), ())),
                    preferred_element_type=jnp.float32,
                ).astype(jnp.bfloat16)
                at = pl.ds(pl.multiple_of(block * BS, BS), BS)
                for s in range(2):
                    for h in range(2):
                        prod[2 * g + h, s * BS : (s + 1) * BS, at] = res[
                            h * BS : (h + 1) * BS, s * BS : (s + 1) * BS
                        ]
        return carry

    lax.fori_loop(0, (count + 1) >> 1, one_group, 0)

    def tile(at, span, k):
        left = jnp.dot(prod[at], occ_ref[:, span], preferred_element_type=jnp.float32)
        left = left.astype(jnp.bfloat16).astype(jnp.float32)
        left = [left[s * BS : (s + 1) * BS, :].T for s in range(2)]

        def add(q, center):
            center = center.astype(jnp.float32)
            for s in range(2):
                acc[s, q] += (left[s] * center).reshape(BS // 8, 8, BS).sum(axis=0)

        if n_centers == 1:
            lax.fori_loop(0, n_q, lambda q, x: (add(q, c_refs[0][q, k, span, :]), x)[1], 0)
        else:
            for step, c_ref in zip([0, 1, 2 | plane, 3 ^ plane], c_refs):
                add(aux_at ^ step, c_ref[k, span, :])

    for i in range(blocks_here // 2):
        tile(i, pl.ds(pl.multiple_of((2 * i + parity) * BS, BS), BS), 0)
    for k in range(1, KN):
        for b in range(blocks_here):

            @pl.when(used(b, k))
            def _(b=b, k=k):
                tile(place[column(b, k)], slice(b * BS, (b + 1) * BS), k)

    for s in range(2):
        out_ref[s] = acc[s].sum(axis=1)


def on_device(sizes, three_center, virt_density, occ_density, partner_list, partner_count):
    groups, aux, atoms = sizes
    rows = three_center.shape[0]
    basis_total = virt_density.shape[1]
    group_at = lax.axis_index("groups")
    aux_at = lax.axis_index("aux")
    atom_at = lax.axis_index("atoms")
    where = jnp.stack([atom_at, aux_at & 1, group_at, aux_at]).astype(jnp.int32)
    columns = basis_total // 2
    n_blocks = columns // BS

    core = functools.partial(swap, axes=("atoms",), sizes=(atoms,), move=lambda t: (t ^ 1,))
    across = functools.partial(swap, axes=("atoms",), sizes=(atoms,), move=lambda t: (t ^ 2,))
    plane = functools.partial(swap, axes=("groups",), sizes=(groups,), move=lambda g: (g ^ 1,))
    pair = functools.partial(swap, axes=("aux",), sizes=(aux,), move=lambda a: (a ^ 1,))

    anywhere = pl.BlockSpec(memory_space=pltpu.HBM)
    scalars = pl.BlockSpec(memory_space=pltpu.SMEM)
    vmem = pl.BlockSpec(memory_space=pltpu.VMEM)

    centers = three_center[:, 0].transpose(1, 0, 2)
    far_a = across(centers)
    other = pair(centers)
    mine = pl.pallas_call(
        functools.partial(select, n_blocks),
        out_shape=jax.ShapeDtypeStruct((columns, rows), jnp.bfloat16),
        in_specs=[scalars, anywhere],
        out_specs=vmem,
        scratch_shapes=[
            pltpu.VMEM((n_blocks, rows, BS), jnp.bfloat16),
            pltpu.SemaphoreType.DMA((n_blocks,)),
        ],
        compiler_params=pltpu.CompilerParams(vmem_limit_bytes=8 * MIB),
    )(where, virt_density)
    v_across = across(mine)
    counts = core(after(partner_count, far_a))
    if aux == 4:
        rest_a = swap(centers, ("groups", "aux"), (groups, aux), lambda g, a: (g, a ^ (2 | g)))
        rest_b = plane(rest_a)
        all_centers = [centers, other, rest_a, rest_b]
        far_b = pair(after(far_a, other, rest_a, counts))
    else:
        all_centers = [lax.all_gather(centers, "aux", axis=0)]
        far_b = pair(after(far_a, other))

    m_parts = [centers, core(centers), far_a, core(far_a), other, core(other), far_b]
    m_parts.append(core(far_b))
    mine_core = core(mine)
    moved = core(after(v_across, *m_parts[1:], all_centers[-1], mine_core))
    v_parts = [mine, mine_core, v_across, moved]
    sums = pl.pallas_call(
        functools.partial(contract, len(all_centers)),
        out_shape=jax.ShapeDtypeStruct((2, aux, BS), jnp.float32),
        in_specs=[scalars] * 3 + [vmem] * (13 + len(all_centers)),
        out_specs=vmem,
        scratch_shapes=[
            pltpu.VMEM((n_blocks, 2 * BS, basis_total), jnp.bfloat16),
            pltpu.VMEM((2, aux, 8, BS), jnp.float32),
            pltpu.SMEM((n_blocks,), jnp.int32),
            pltpu.SMEM((n_blocks,), jnp.int32),
        ],
        compiler_params=pltpu.CompilerParams(vmem_limit_bytes=(24 if aux == 4 else 48) * MIB),
    )(where, partner_list.T, counts, *v_parts, *m_parts, occ_density, *all_centers)

    sums = sums + core(sums)
    diagonal = swap(sums[1], ("aux", "atoms"), (aux, atoms), lambda a, t: (a ^ 1, t ^ 2))
    total = sums[0] + across(sums[0]) + pair(sums[1]) + diagonal
    share = aux // atoms
    row = lax.dynamic_slice_in_dim(total, atom_at * share, share, 0)
    return (row.sum(axis=1) * jnp.float32(-(basis_total ** (-0.5))))[None, :]


def solution(mesh):
    sizes = tuple(mesh.shape[name] for name in ("groups", "aux", "atoms"))
    in_specs = (
        P("atoms", "aux", None, None),
        P(("groups", "atoms"), None),
        P("groups", "atoms"),
        P(),
        P(),
    )
    out_specs = P(("groups", "aux"), "atoms")
    return jax.shard_map(
        functools.partial(on_device, sizes),
        mesh=mesh,
        in_specs=in_specs,
        out_specs=out_specs,
        check_vma=False,
    )
```

profile of v0, /device:TPU:0, one launch (start us, length us, event | category | flops | bytes accessed | tf_op | source)
XLA Modules:
  0.0 57.4 jit_solution(4071738238377515697)
XLA Ops:
  0.0 0.0 copy-start.4
  0.0 0.0 copy-start.3
  0.0 2.9 %collective-permute-start = (bf16[3,512,128]{2,1,0:T(8,128)(2,1)}, bf16[3,512,128]{2,1,0:T(8,128)(2,1)S(1)}, u32[]{:S(2)}, u32[]{:S(2)}) collective-permute-start(bf16[3,512,128]{2,1,0:T(8,128)(2,1)} %bitcast.15), channel_id=1, source_target_pairs={{0,2},{1,3},{2,0},{3,1},{4,6},{5,7},{6,4},{7,5},{8,10},{9,11},{10,... | collective-permute-start | bytes 1179656 | tf_op jit(solution)/shard_map/ppermute | solution.py:29
  2.9 2.6 %collective-permute-start.8 = (bf16[3,512,128]{2,1,0:T(8,128)(2,1)}, bf16[3,512,128]{2,1,0:T(8,128)(2,1)S(1)}, u32[]{:S(2)}, u32[]{:S(2)}) collective-permute-start(bf16[3,512,128]{2,1,0:T(8,128)(2,1)} %bitcast.16), channel_id=1, source_target_pairs={{0,8},{4,12},{8,0},{12,4},{16,28},{20,24},{24,20},{28,16},{1,9},{5... | collective-permute-start | bytes 1179656 | tf_op jit(solution)/shard_map/ppermute | solution.py:29
  5.5 1.6 %collective-permute-start.6 = (bf16[3,512,128]{2,1,0:T(8,128)(2,1)}, bf16[3,512,128]{2,1,0:T(8,128)(2,1)S(1)}, u32[]{:S(2)}, u32[]{:S(2)}) collective-permute-start(bf16[3,512,128]{2,1,0:T(8,128)(2,1)} %bitcast.17), channel_id=1, source_target_pairs={{0,4},{4,0},{8,12},{12,8},{1,5},{5,1},{9,13},{13,9},{2,6},{6,2},{1... | collective-permute-start | bytes 1179656 | tf_op jit(solution)/shard_map/ppermute | solution.py:29
  7.1 0.1 pad_add_fusion.where
  7.2 0.0 copy-start
  7.2 1.6 %copy-done = bf16[512,2048]{1,0:T(8,128)(2,1)S(1)} copy-done((bf16[512,2048]{1,0:T(8,128)(2,1)S(1)}, bf16[512,2048]{1,0:T(8,128)(2,1)}, u32[]{:S(2)}) %copy-start) | copy-done | bytes 2097176
  8.8 0.0 copy-start.2
  8.8 0.0 copy-start.1
  8.8 1.6 %shard_map.55.refs_0_ = bf16[1024,512]{1,0:T(8,128)(2,1)S(1)} custom-call(s32[4]{0:T(128)S(1)} %pad_add_fusion.where, bf16[512,2048]{1,0:T(8,128)(2,1)S(1)} %copy-done), custom_call_target="tpu_custom_call" | custom-call | tf_op jit(solution)/shard_map/pallas_call | solution.py:176
  10.4 0.6 %collective-permute-start.3 = (bf16[1024,512]{1,0:T(8,128)(2,1)S(1)}, bf16[1024,512]{1,0:T(8,128)(2,1)S(1)}, u32[]{:S(2)}, u32[]{:S(2)}) collective-permute-start(bf16[1024,512]{1,0:T(8,128)(2,1)S(1)} %shard_map.55.refs_0_), channel_id=1, source_target_pairs={{0,2},{1,3},{2,0},{3,1},{4,6},{5,7},{6,4},{7,5},{8,10},{9,11},{10,... | collective-permute-start | bytes 3145736 | tf_op jit(solution)/shard_map/ppermute | solution.py:29
  11.0 0.0 collective-permute-start.2
  11.0 1.7 %collective-permute-done.refs_6_ = bf16[3,512,128]{2,1,0:T(8,128)(2,1)S(1)} collective-permute-done((bf16[3,512,128]{2,1,0:T(8,128)(2,1)}, bf16[3,512,128]{2,1,0:T(8,128)(2,1)S(1)}, u32[]{:S(2)}, u32[]{:S(2)}) %collective-permute-start) | collective-permute-done | bytes 393248 | tf_op jit(solution)/shard_map/ppermute | solution.py:29
  12.8 0.0 copy-done.2
  12.8 0.0 collective-permute-start.4
  12.8 10.4 %collective-permute-done.8.refs_15_ = bf16[3,512,128]{2,1,0:T(8,128)(2,1)S(1)} collective-permute-done((bf16[3,512,128]{2,1,0:T(8,128)(2,1)}, bf16[3,512,128]{2,1,0:T(8,128)(2,1)S(1)}, u32[]{:S(2)}, u32[]{:S(2)}) %collective-permute-start.8) | collective-permute-done | bytes 393248 | tf_op jit(solution)/shard_map/ppermute | solution.py:29
  23.2 0.0 copy-done.4
  23.2 0.0 collective-permute-start.1
  23.2 0.2 collective-permute-done.6.refs_8_.refs_14_
  23.4 2.3 %collective-permute-start.11 = (bf16[3,512,128]{2,1,0:T(8,128)(2,1)S(1)}, bf16[3,512,128]{2,1,0:T(8,128)(2,1)S(1)}, u32[]{:S(2)}, u32[]{:S(2)}) collective-permute-start(bf16[3,512,128]{2,1,0:T(8,128)(2,1)S(1)} %collective-permute-done.8.refs_15_), channel_id=1, source_target_pairs={{0,16},{16,0},{1,17},{17,1},{2,18},{18,2},{3,19},{19,3},{4,20},{20... | collective-permute-start | bytes 1179656 | tf_op jit(solution)/shard_map/ppermute | solution.py:29
  25.7 0.0 collective-permute-done.1.pcount
  25.7 1.7 %collective-permute-start.9 = (bf16[3,512,128]{2,1,0:T(8,128)(2,1)S(1)}, bf16[3,512,128]{2,1,0:T(8,128)(2,1)S(1)}, u32[]{:S(2)}, u32[]{:S(2)}) collective-permute-start(bf16[3,512,128]{2,1,0:T(8,128)(2,1)S(1)} %collective-permute-done.refs_6_), channel_id=1, source_target_pairs={{0,4},{4,0},{8,12},{12,8},{1,5},{5,1},{9,13},{13,9},{2,6},{6,2},{1... | collective-permute-start | bytes 1179656 | tf_op jit(solution)/shard_map/ppermute | solution.py:29
  27.3 0.0 collective-permute-done.4.refs_5_
  27.3 0.0 collective-permute-start.7
  27.3 7.6 %collective-permute-done.11.refs_16_ = bf16[3,512,128]{2,1,0:T(8,128)(2,1)S(1)} collective-permute-done((bf16[3,512,128]{2,1,0:T(8,128)(2,1)S(1)}, bf16[3,512,128]{2,1,0:T(8,128)(2,1)S(1)}, u32[]{:S(2)}, u32[]{:S(2)}) %collective-permute-start.11) | collective-permute-done | bytes 393248 | tf_op jit(solution)/shard_map/ppermute | solution.py:29
  35.0 0.0 collective-permute-start.5
  35.0 1.5 %collective-permute-done.9.refs_10_ = bf16[3,512,128]{2,1,0:T(8,128)(2,1)S(1)} collective-permute-done((bf16[3,512,128]{2,1,0:T(8,128)(2,1)S(1)}, bf16[3,512,128]{2,1,0:T(8,128)(2,1)S(1)}, u32[]{:S(2)}, u32[]{:S(2)}) %collective-permute-start.9) | collective-permute-done | bytes 393248 | tf_op jit(solution)/shard_map/ppermute | solution.py:29
  36.4 0.0 collective-permute-start.10
  36.4 0.0 collective-permute-done.7.refs_9_
  36.4 0.2 collective-permute-done.5.refs_7_
  36.7 0.0 collective-permute-done.3.refs_2_
  36.7 0.0 collective-permute-done.2.refs_1_
  36.7 1.5 %collective-permute-done.10.refs_11_ = bf16[3,512,128]{2,1,0:T(8,128)(2,1)S(1)} collective-permute-done((bf16[3,512,128]{2,1,0:T(8,128)(2,1)S(1)}, bf16[3,512,128]{2,1,0:T(8,128)(2,1)S(1)}, u32[]{:S(2)}, u32[]{:S(2)}) %collective-permute-start.10) | collective-permute-done | bytes 393248 | tf_op jit(solution)/shard_map/ppermute | solution.py:29
  38.2 0.1 collective-permute-start.12
  38.3 2.5 %collective-permute-done.12.refs_3_ = bf16[1024,512]{1,0:T(8,128)(2,1)S(1)} collective-permute-done((bf16[1024,512]{1,0:T(8,128)(2,1)S(1)}, bf16[1024,512]{1,0:T(8,128)(2,1)S(1)}, u32[]{:S(2)}, u32[]{:S(2)}) %collective-permute-start.12) | collective-permute-done | bytes 1048608 | tf_op jit(solution)/shard_map/ppermute | solution.py:29
  40.8 0.0 copy-done.3
  40.8 0.0 copy-done.1
  40.8 6.3 %shard_map.56 = f32[2,4,128]{2,1,0:T(4,128)S(1)} custom-call(s32[4]{0:T(128)S(1)} %pad_add_fusion.where, s32[3,16]{1,0:T(4,128)S(1)} %bitcast.21, s32[16]{0:T(128)S(1)} %collective-permute-done.1.pcount, bf16[1024,512]{1,0:T(8,128)(2,1)S(1)} %shard_map.55.refs_0_, bf16[1024,512]{1,0:T(8,128)(2,1)S(1)} %collective-permute-done.2.refs_1_, ...), custom_call_target="tpu_custom_call" | custom-call | tf_op jit(solution)/shard_map/pallas_call | solution.py:203
  47.1 2.6 %collective-permute-start.13 = (f32[2,4,128]{2,1,0:T(4,128)S(1)}, f32[2,4,128]{2,1,0:T(4,128)S(1)}, u32[]{:S(2)}, u32[]{:S(2)}) collective-permute-start(f32[2,4,128]{2,1,0:T(4,128)S(1)} %shard_map.56), channel_id=1, source_target_pairs={{0,1},{1,0},{2,3},{3,2},{4,5},{5,4},{6,7},{7,6},{8,9},{9,8},{10,11... | collective-permute-start | bytes 12296 | tf_op jit(solution)/shard_map/ppermute | solution.py:29
  49.7 0.8 %collective-permute-done.13 = f32[2,4,128]{2,1,0:T(4,128)S(1)} collective-permute-done((f32[2,4,128]{2,1,0:T(4,128)S(1)}, f32[2,4,128]{2,1,0:T(4,128)S(1)}, u32[]{:S(2)}, u32[]{:S(2)}) %collective-permute-start.13) | collective-permute-done | bytes 4128 | tf_op jit(solution)/shard_map/ppermute | solution.py:29
  50.5 0.0 collective-permute-start.14
  50.5 0.1 collective-permute-start.16
  50.6 3.4 %collective-permute-start.15 = (f32[4,128]{1,0:T(4,128)S(1)}, f32[4,128]{1,0:T(4,128)S(1)}, u32[]{:S(2)}, u32[]{:S(2)}) collective-permute-start(f32[4,128]{1,0:T(4,128)S(1)} %get-tuple-element.12), channel_id=1, source_target_pairs={{0,4},{4,0},{8,12},{12,8},{1,5},{5,1},{9,13},{13,9},{2,6},{6,2},{1... | collective-permute-start | bytes 6152 | tf_op jit(solution)/shard_map/ppermute | solution.py:29
  54.0 0.1 collective-permute-done.14
  54.1 1.0 %collective-permute-done.16 = f32[4,128]{1,0:T(4,128)S(1)} collective-permute-done((f32[4,128]{1,0:T(4,128)S(1)}, f32[4,128]{1,0:T(4,128)S(1)}, u32[]{:S(2)}, u32[]{:S(2)}) %collective-permute-start.16) | collective-permute-done | bytes 2080 | tf_op jit(solution)/shard_map/ppermute | solution.py:29
  55.1 0.5 collective-permute-done.15
  55.6 0.6 %dynamic-slice_reduce_fusion = f32[]{:T(128)} fusion(f32[4,128]{1,0:T(4,128)S(1)} %add_add_fusion, s32[]{:T(128)S(6)} %select_n.3), kind=kLoop, calls=%fused_computation.4 | loop fusion | flops 127 | bytes 520 | tf_op jit(solution)/shard_map/reduce_sum | solution.py:222
  (3 shorter events, 0.0 us)
Async XLA Ops:
  0.0 23.2 %copy-start.4 = (s32[16]{0:T(128)S(1)}, s32[16]{0:T(128)}, u32[]{:S(2)}) copy-start(s32[16]{0:T(128)} %param.9) | copy-start | bytes 196
  0.0 40.8 %copy-start.3 = (s32[16,3]{0,1:T(4,128)S(1)}, s32[16,3]{0,1:T(4,128)}, u32[]{:S(2)}) copy-start(s32[16,3]{0,1:T(4,128)} %param.8) | copy-start | bytes 580
  0.0 12.8 %collective-permute-start = (bf16[3,512,128]{2,1,0:T(8,128)(2,1)}, bf16[3,512,128]{2,1,0:T(8,128)(2,1)S(1)}, u32[]{:S(2)}, u32[]{:S(2)}) collective-permute-start(bf16[3,512,128]{2,1,0:T(8,128)(2,1)} %bitcast.15), channel_id=1, source_target_pairs={{0,2},{1,3},{2,0},{3,1},{4,6},{5,7},{6,4},{7,5},{8,10},{9,11},{10,... | collective-permute-start | bytes 1179656 | tf_op jit(solution)/shard_map/ppermute | solution.py:29
  2.9 20.2 %collective-permute-start.8 = (bf16[3,512,128]{2,1,0:T(8,128)(2,1)}, bf16[3,512,128]{2,1,0:T(8,128)(2,1)S(1)}, u32[]{:S(2)}, u32[]{:S(2)}) collective-permute-start(bf16[3,512,128]{2,1,0:T(8,128)(2,1)} %bitcast.16), channel_id=1, source_target_pairs={{0,8},{4,12},{8,0},{12,4},{16,28},{20,24},{24,20},{28,16},{1,9},{5... | collective-permute-start | bytes 1179656 | tf_op jit(solution)/shard_map/ppermute | solution.py:29
  5.5 17.8 %collective-permute-start.6 = (bf16[3,512,128]{2,1,0:T(8,128)(2,1)}, bf16[3,512,128]{2,1,0:T(8,128)(2,1)S(1)}, u32[]{:S(2)}, u32[]{:S(2)}) collective-permute-start(bf16[3,512,128]{2,1,0:T(8,128)(2,1)} %bitcast.17), channel_id=1, source_target_pairs={{0,4},{4,0},{8,12},{12,8},{1,5},{5,1},{9,13},{13,9},{2,6},{6,2},{1... | collective-permute-start | bytes 1179656 | tf_op jit(solution)/shard_map/ppermute | solution.py:29
  7.2 1.6 %copy-start = (bf16[512,2048]{1,0:T(8,128)(2,1)S(1)}, bf16[512,2048]{1,0:T(8,128)(2,1)}, u32[]{:S(2)}) copy-start(bf16[512,2048]{1,0:T(8,128)(2,1)} %virt_ref.1) | copy-start | bytes 6291460
  8.8 4.0 %copy-start.2 = (bf16[512,1,3,128]{3,0,2,1:T(8,128)(2,1)S(1)}, bf16[512,1,3,128]{3,0,2,1:T(8,128)(2,1)}, u32[]{:S(2)}) copy-start(bf16[512,1,3,128]{3,0,2,1:T(8,128)(2,1)} %param.5) | copy-start | bytes 1179652
  8.8 32.0 %copy-start.1 = (bf16[2048,512]{1,0:T(8,128)(2,1)S(1)}, bf16[2048,512]{1,0:T(8,128)(2,1)}, u32[]{:S(2)}) copy-start(bf16[2048,512]{1,0:T(8,128)(2,1)} %refs_12_.1) | copy-start | bytes 6291460
  10.4 26.3 %collective-permute-start.3 = (bf16[1024,512]{1,0:T(8,128)(2,1)S(1)}, bf16[1024,512]{1,0:T(8,128)(2,1)S(1)}, u32[]{:S(2)}, u32[]{:S(2)}) collective-permute-start(bf16[1024,512]{1,0:T(8,128)(2,1)S(1)} %shard_map.55.refs_0_), channel_id=1, source_target_pairs={{0,2},{1,3},{2,0},{3,1},{4,6},{5,7},{6,4},{7,5},{8,10},{9,11},{10,... | collective-permute-start | bytes 3145736 | tf_op jit(solution)/shard_map/ppermute | solution.py:29
  11.0 25.7 %collective-permute-start.2 = (bf16[1024,512]{1,0:T(8,128)(2,1)S(1)}, bf16[1024,512]{1,0:T(8,128)(2,1)S(1)}, u32[]{:S(2)}, u32[]{:S(2)}) collective-permute-start(bf16[1024,512]{1,0:T(8,128)(2,1)S(1)} %shard_map.55.refs_0_), channel_id=1, source_target_pairs={{0,1},{1,0},{2,3},{3,2},{4,5},{5,4},{6,7},{7,6},{8,9},{9,8},{10,11... | collective-permute-start | bytes 3145736 | tf_op jit(solution)/shard_map/ppermute | solution.py:29
  12.8 14.5 %collective-permute-start.4 = (bf16[3,512,128]{2,1,0:T(8,128)(2,1)S(1)}, bf16[3,512,128]{2,1,0:T(8,128)(2,1)S(1)}, u32[]{:S(2)}, u32[]{:S(2)}) collective-permute-start(bf16[3,512,128]{2,1,0:T(8,128)(2,1)S(1)} %bitcast.18), channel_id=1, source_target_pairs={{0,1},{1,0},{2,3},{3,2},{4,5},{5,4},{6,7},{7,6},{8,9},{9,8},{10,11... | collective-permute-start | bytes 1179656 | tf_op jit(solution)/shard_map/ppermute | solution.py:29
  23.2 2.5 %collective-permute-start.1 = (s32[16]{0:T(128)S(1)}, s32[16]{0:T(128)S(1)}, u32[]{:S(2)}, u32[]{:S(2)}) collective-permute-start(s32[16]{0:T(128)S(1)} %copy-done.4), channel_id=1, source_target_pairs={{0,1},{1,0},{2,3},{3,2},{4,5},{5,4},{6,7},{7,6},{8,9},{9,8},{10,11... | collective-permute-start | bytes 200 | tf_op jit(solution)/shard_map/ppermute | solution.py:29
  23.4 11.6 %collective-permute-start.11 = (bf16[3,512,128]{2,1,0:T(8,128)(2,1)S(1)}, bf16[3,512,128]{2,1,0:T(8,128)(2,1)S(1)}, u32[]{:S(2)}, u32[]{:S(2)}) collective-permute-start(bf16[3,512,128]{2,1,0:T(8,128)(2,1)S(1)} %collective-permute-done.8.refs_15_), channel_id=1, source_target_pairs={{0,16},{16,0},{1,17},{17,1},{2,18},{18,2},{3,19},{19,3},{4,20},{20... | collective-permute-start | bytes 1179656 | tf_op jit(solution)/shard_map/ppermute | solution.py:29
  25.7 10.8 %collective-permute-start.9 = (bf16[3,512,128]{2,1,0:T(8,128)(2,1)S(1)}, bf16[3,512,128]{2,1,0:T(8,128)(2,1)S(1)}, u32[]{:S(2)}, u32[]{:S(2)}) collective-permute-start(bf16[3,512,128]{2,1,0:T(8,128)(2,1)S(1)} %collective-permute-done.refs_6_), channel_id=1, source_target_pairs={{0,4},{4,0},{8,12},{12,8},{1,5},{5,1},{9,13},{13,9},{2,6},{6,2},{1... | collective-permute-start | bytes 1179656 | tf_op jit(solution)/shard_map/ppermute | solution.py:29
  27.3 9.1 %collective-permute-start.7 = (bf16[3,512,128]{2,1,0:T(8,128)(2,1)S(1)}, bf16[3,512,128]{2,1,0:T(8,128)(2,1)S(1)}, u32[]{:S(2)}, u32[]{:S(2)}) collective-permute-start(bf16[3,512,128]{2,1,0:T(8,128)(2,1)S(1)} %collective-permute-done.6.refs_8_.refs_14_), channel_id=1, source_target_pairs={{0,1},{1,0},{2,3},{3,2},{4,5},{5,4},{6,7},{7,6},{8,9},{9,8},{10,11... | collective-permute-start | bytes 1179656 | tf_op jit(solution)/shard_map/ppermute | solution.py:29
  35.0 1.7 %collective-permute-start.5 = (bf16[3,512,128]{2,1,0:T(8,128)(2,1)S(1)}, bf16[3,512,128]{2,1,0:T(8,128)(2,1)S(1)}, u32[]{:S(2)}, u32[]{:S(2)}) collective-permute-start(bf16[3,512,128]{2,1,0:T(8,128)(2,1)S(1)} %collective-permute-done.refs_6_), channel_id=1, source_target_pairs={{0,1},{1,0},{2,3},{3,2},{4,5},{5,4},{6,7},{7,6},{8,9},{9,8},{10,11... | collective-permute-start | bytes 1179656 | tf_op jit(solution)/shard_map/ppermute | solution.py:29
  36.4 1.7 %collective-permute-start.10 = (bf16[3,512,128]{2,1,0:T(8,128)(2,1)S(1)}, bf16[3,512,128]{2,1,0:T(8,128)(2,1)S(1)}, u32[]{:S(2)}, u32[]{:S(2)}) collective-permute-start(bf16[3,512,128]{2,1,0:T(8,128)(2,1)S(1)} %collective-permute-done.9.refs_10_), channel_id=1, source_target_pairs={{0,1},{1,0},{2,3},{3,2},{4,5},{5,4},{6,7},{7,6},{8,9},{9,8},{10,11... | collective-permute-start | bytes 1179656 | tf_op jit(solution)/shard_map/ppermute | solution.py:29
  38.2 2.7 %collective-permute-start.12 = (bf16[1024,512]{1,0:T(8,128)(2,1)S(1)}, bf16[1024,512]{1,0:T(8,128)(2,1)S(1)}, u32[]{:S(2)}, u32[]{:S(2)}) collective-permute-start(bf16[1024,512]{1,0:T(8,128)(2,1)S(1)} %collective-permute-done.3.refs_2_), channel_id=1, source_target_pairs={{0,1},{1,0},{2,3},{3,2},{4,5},{5,4},{6,7},{7,6},{8,9},{9,8},{10,11... | collective-permute-start | bytes 3145736 | tf_op jit(solution)/shard_map/ppermute | solution.py:29
  47.1 3.4 %collective-permute-start.13 = (f32[2,4,128]{2,1,0:T(4,128)S(1)}, f32[2,4,128]{2,1,0:T(4,128)S(1)}, u32[]{:S(2)}, u32[]{:S(2)}) collective-permute-start(f32[2,4,128]{2,1,0:T(4,128)S(1)} %shard_map.56), channel_id=1, source_target_pairs={{0,1},{1,0},{2,3},{3,2},{4,5},{5,4},{6,7},{7,6},{8,9},{9,8},{10,11... | collective-permute-start | bytes 12296 | tf_op jit(solution)/shard_map/ppermute | solution.py:29
  50.5 3.6 %collective-permute-start.14 = (f32[4,128]{1,0:T(4,128)S(1)}, f32[4,128]{1,0:T(4,128)S(1)}, u32[]{:S(2)}, u32[]{:S(2)}) collective-permute-start(f32[4,128]{1,0:T(4,128)S(1)} %get-tuple-element.11), channel_id=1, source_target_pairs={{0,2},{1,3},{2,0},{3,1},{4,6},{5,7},{6,4},{7,5},{8,10},{9,11},{10,... | collective-permute-start | bytes 6152 | tf_op jit(solution)/shard_map/ppermute | solution.py:29
  50.5 4.5 %collective-permute-start.16 = (f32[4,128]{1,0:T(4,128)S(1)}, f32[4,128]{1,0:T(4,128)S(1)}, u32[]{:S(2)}, u32[]{:S(2)}) collective-permute-start(f32[4,128]{1,0:T(4,128)S(1)} %get-tuple-element.12), channel_id=1, source_target_pairs={{0,6},{1,7},{2,4},{3,5},{4,2},{5,3},{6,0},{7,1},{8,14},{9,15},{10,... | collective-permute-start | bytes 6152 | tf_op jit(solution)/shard_map/ppermute | solution.py:29
  50.6 5.0 %collective-permute-start.15 = (f32[4,128]{1,0:T(4,128)S(1)}, f32[4,128]{1,0:T(4,128)S(1)}, u32[]{:S(2)}, u32[]{:S(2)}) collective-permute-start(f32[4,128]{1,0:T(4,128)S(1)} %get-tuple-element.12), channel_id=1, source_target_pairs={{0,4},{4,0},{8,12},{12,8},{1,5},{5,1},{9,13},{13,9},{2,6},{6,2},{1... | collective-permute-start | bytes 6152 | tf_op jit(solution)/shard_map/ppermute | solution.py:29
where the time goes:
time: 57.8 us; the launch traced here: 57.4 us
  waiting for transfers between devices  28 us (48%)
  starting transfers between devices  17.9 us (31%)
  Pallas kernels  7.93 us (14%)
  local copies, waits for them, and re-layouts  1.61 us (3%)
  between operations  1.21 us (2%)
  other arithmetic  0.69 us (1%)
    ppermute x17, waiting for transfers between devices, swap(): return lax.ppermute(x, axes, perm)  28 us
    ppermute x17, starting transfers between devices, swap(): return lax.ppermute(x, axes, perm)  17.9 us
    pallas_call x1, Pallas kernels, on_device(): pl.pallas_call(functools.partial(contract, len(all_centers)), out_shape=j...  6.29 us
    pallas_call x1, Pallas kernels, on_device(): pl.pallas_call(functools.partial(select, n_blocks), out_shape=jax.ShapeDt...  1.64 us
    unnamed x10, local copies, waits for them, and re-layouts  1.61 us
  transfers between devices with their start and end apart: 17, of which 12 were waited for; matrix products, arithmetic and copies ran while one was open for 0% of the time, Pallas kernels for 3%

commit v1 on v0

--- a/solution.py
+++ b/solution.py
@@ -188,7 +188,7 @@
     counts = core(after(partner_count, far_a))
     if aux == 4:
         rest_a = swap(centers, ("groups", "aux"), (groups, aux), lambda g, a: (g, a ^ (2 | g)))
-        rest_b = plane(rest_a)
+        rest_b = plane(after(rest_a, counts))
         all_centers = [centers, other, rest_a, rest_b]
         far_b = pair(after(far_a, other, rest_a, counts))
     else:

time: 57.8 us -> 56.2 us (0.972)
  starting transfers between devices: 17.9 us -> 15 us
  waiting for transfers between devices: 28 us -> 29.5 us
    ppermute x17, starting transfers between devices: 17.9 us -> 15 us  [swap(): return lax.ppermute(x, axes, perm)]
    ppermute x17, waiting for transfers between devices: 28 us -> 29.5 us  [swap(): return lax.ppermute(x, axes, perm)]
where the time goes in v1:
time: 56.2 us; the launch traced here: 55.9 us
  waiting for transfers between devices  29.5 us (52%)
  starting transfers between devices  15 us (27%)
  Pallas kernels  7.96 us (14%)
  local copies, waits for them, and re-layouts  1.61 us (3%)
  between operations  1.21 us (2%)
  other arithmetic  0.69 us (1%)
    ppermute x17, waiting for transfers between devices, swap(): return lax.ppermute(x, axes, perm)  29.5 us
    ppermute x17, starting transfers between devices, swap(): return lax.ppermute(x, axes, perm)  15 us
    pallas_call x1, Pallas kernels, on_device(): pl.pallas_call(functools.partial(contract, len(all_centers)), out_shape=j...  6.31 us
    pallas_call x1, Pallas kernels, on_device(): pl.pallas_call(functools.partial(select, n_blocks), out_shape=jax.ShapeDt...  1.64 us
    unnamed x10, local copies, waits for them, and re-layouts  1.61 us
  transfers between devices with their start and end apart: 17, of which 12 were waited for; matrix products, arithmetic and copies ran while one was open for 0% of the time, Pallas kernels for 3%

profile of v1, /device:TPU:0, one launch (start us, length us, event | category | flops | bytes accessed | tf_op | source)
XLA Modules:
  0.0 55.9 jit_solution(5166151350365158315)
XLA Ops:
  0.0 0.0 copy-start.4
  0.0 0.0 copy-start.3
  0.0 2.9 %collective-permute-start = (bf16[3,512,128]{2,1,0:T(8,128)(2,1)}, bf16[3,512,128]{2,1,0:T(8,128)(2,1)S(1)}, u32[]{:S(2)}, u32[]{:S(2)}) collective-permute-start(bf16[3,512,128]{2,1,0:T(8,128)(2,1)} %bitcast.15), channel_id=1, source_target_pairs={{0,2},{1,3},{2,0},{3,1},{4,6},{5,7},{6,4},{7,5},{8,10},{9,11},{10,... | collective-permute-start | bytes 1179656 | tf_op jit(solution)/shard_map/ppermute | solution.py:29
  2.9 2.6 %collective-permute-start.8 = (bf16[3,512,128]{2,1,0:T(8,128)(2,1)}, bf16[3,512,128]{2,1,0:T(8,128)(2,1)S(1)}, u32[]{:S(2)}, u32[]{:S(2)}) collective-permute-start(bf16[3,512,128]{2,1,0:T(8,128)(2,1)} %bitcast.16), channel_id=1, source_target_pairs={{0,8},{4,12},{8,0},{12,4},{16,28},{20,24},{24,20},{28,16},{1,9},{5... | collective-permute-start | bytes 1179656 | tf_op jit(solution)/shard_map/ppermute | solution.py:29
  5.5 1.6 %collective-permute-start.6 = (bf16[3,512,128]{2,1,0:T(8,128)(2,1)}, bf16[3,512,128]{2,1,0:T(8,128)(2,1)S(1)}, u32[]{:S(2)}, u32[]{:S(2)}) collective-permute-start(bf16[3,512,128]{2,1,0:T(8,128)(2,1)} %bitcast.17), channel_id=1, source_target_pairs={{0,4},{4,0},{8,12},{12,8},{1,5},{5,1},{9,13},{13,9},{2,6},{6,2},{1... | collective-permute-start | bytes 1179656 | tf_op jit(solution)/shard_map/ppermute | solution.py:29
  7.1 0.1 pad_add_fusion.where
  7.2 0.0 copy-start
  7.2 1.6 %copy-done = bf16[512,2048]{1,0:T(8,128)(2,1)S(1)} copy-done((bf16[512,2048]{1,0:T(8,128)(2,1)S(1)}, bf16[512,2048]{1,0:T(8,128)(2,1)}, u32[]{:S(2)}) %copy-start) | copy-done | bytes 2097176
  8.8 0.0 copy-start.2
  8.8 0.0 copy-start.1
  8.8 1.6 %shard_map.55.refs_0_ = bf16[1024,512]{1,0:T(8,128)(2,1)S(1)} custom-call(s32[4]{0:T(128)S(1)} %pad_add_fusion.where, bf16[512,2048]{1,0:T(8,128)(2,1)S(1)} %copy-done), custom_call_target="tpu_custom_call" | custom-call | tf_op jit(solution)/shard_map/pallas_call | solution.py:176
  10.4 0.6 %collective-permute-start.3 = (bf16[1024,512]{1,0:T(8,128)(2,1)S(1)}, bf16[1024,512]{1,0:T(8,128)(2,1)S(1)}, u32[]{:S(2)}, u32[]{:S(2)}) collective-permute-start(bf16[1024,512]{1,0:T(8,128)(2,1)S(1)} %shard_map.55.refs_0_), channel_id=1, source_target_pairs={{0,2},{1,3},{2,0},{3,1},{4,6},{5,7},{6,4},{7,5},{8,10},{9,11},{10,... | collective-permute-start | bytes 3145736 | tf_op jit(solution)/shard_map/ppermute | solution.py:29
  11.0 0.0 collective-permute-start.2
  11.0 1.7 %collective-permute-done.refs_6_ = bf16[3,512,128]{2,1,0:T(8,128)(2,1)S(1)} collective-permute-done((bf16[3,512,128]{2,1,0:T(8,128)(2,1)}, bf16[3,512,128]{2,1,0:T(8,128)(2,1)S(1)}, u32[]{:S(2)}, u32[]{:S(2)}) %collective-permute-start) | collective-permute-done | bytes 393248 | tf_op jit(solution)/shard_map/ppermute | solution.py:29
  12.8 0.0 copy-done.2
  12.8 0.0 collective-permute-start.4
  12.8 10.4 %collective-permute-done.8.refs_15_ = bf16[3,512,128]{2,1,0:T(8,128)(2,1)S(1)} collective-permute-done((bf16[3,512,128]{2,1,0:T(8,128)(2,1)}, bf16[3,512,128]{2,1,0:T(8,128)(2,1)S(1)}, u32[]{:S(2)}, u32[]{:S(2)}) %collective-permute-start.8) | collective-permute-done | bytes 393248 | tf_op jit(solution)/shard_map/ppermute | solution.py:29
  23.2 0.0 copy-done.4
  23.2 0.0 collective-permute-start.1
  23.2 0.2 collective-permute-done.6.refs_8_.refs_14_
  23.4 0.3 collective-permute-start.7
  23.7 0.6 %collective-permute-done.1.pcount = s32[16]{0:T(128)S(1)} collective-permute-done((s32[16]{0:T(128)S(1)}, s32[16]{0:T(128)S(1)}, u32[]{:S(2)}, u32[]{:S(2)}) %collective-permute-start.1) | collective-permute-done | bytes 96 | tf_op jit(solution)/shard_map/ppermute | solution.py:29
  24.3 0.6 %collective-permute-start.9 = (bf16[3,512,128]{2,1,0:T(8,128)(2,1)S(1)}, bf16[3,512,128]{2,1,0:T(8,128)(2,1)S(1)}, u32[]{:S(2)}, u32[]{:S(2)}) collective-permute-start(bf16[3,512,128]{2,1,0:T(8,128)(2,1)S(1)} %collective-permute-done.refs_6_), channel_id=1, source_target_pairs={{0,4},{4,0},{8,12},{12,8},{1,5},{5,1},{9,13},{13,9},{2,6},{6,2},{1... | collective-permute-start | bytes 1179656 | tf_op jit(solution)/shard_map/ppermute | solution.py:29
  25.0 0.0 collective-permute-done.4.refs_5_
  25.0 0.1 collective-permute-start.5
  25.0 0.0 collective-permute-done.7.refs_9_
  25.1 2.5 %collective-permute-start.11 = (bf16[3,512,128]{2,1,0:T(8,128)(2,1)S(1)}, bf16[3,512,128]{2,1,0:T(8,128)(2,1)S(1)}, u32[]{:S(2)}, u32[]{:S(2)}) collective-permute-start(bf16[3,512,128]{2,1,0:T(8,128)(2,1)S(1)} %collective-permute-done.8.refs_15_), channel_id=1, source_target_pairs={{0,16},{16,0},{1,17},{17,1},{2,18},{18,2},{3,19},{19,3},{4,20},{20... | collective-permute-start | bytes 1179656 | tf_op jit(solution)/shard_map/ppermute | solution.py:29
  27.6 8.0 %collective-permute-done.9.refs_10_ = bf16[3,512,128]{2,1,0:T(8,128)(2,1)S(1)} collective-permute-done((bf16[3,512,128]{2,1,0:T(8,128)(2,1)S(1)}, bf16[3,512,128]{2,1,0:T(8,128)(2,1)S(1)}, u32[]{:S(2)}, u32[]{:S(2)}) %collective-permute-start.9) | collective-permute-done | bytes 393248 | tf_op jit(solution)/shard_map/ppermute | solution.py:29
  35.5 0.0 collective-permute-start.10
  35.5 0.0 collective-permute-done.5.refs_7_
  35.5 1.6 %collective-permute-done.11.refs_16_ = bf16[3,512,128]{2,1,0:T(8,128)(2,1)S(1)} collective-permute-done((bf16[3,512,128]{2,1,0:T(8,128)(2,1)S(1)}, bf16[3,512,128]{2,1,0:T(8,128)(2,1)S(1)}, u32[]{:S(2)}, u32[]{:S(2)}) %collective-permute-start.11) | collective-permute-done | bytes 393248 | tf_op jit(solution)/shard_map/ppermute | solution.py:29
  37.1 0.0 collective-permute-done.3.refs_2_
  37.1 0.0 collective-permute-done.2.refs_1_
  37.1 0.1 collective-permute-done.10.refs_11_
  37.3 0.1 collective-permute-start.12
  37.4 2.5 %collective-permute-done.12.refs_3_ = bf16[1024,512]{1,0:T(8,128)(2,1)S(1)} collective-permute-done((bf16[1024,512]{1,0:T(8,128)(2,1)S(1)}, bf16[1024,512]{1,0:T(8,128)(2,1)S(1)}, u32[]{:S(2)}, u32[]{:S(2)}) %collective-permute-start.12) | collective-permute-done | bytes 1048608 | tf_op jit(solution)/shard_map/ppermute | solution.py:29
  39.9 0.0 copy-done.3
  39.9 0.0 copy-done.1
  39.9 6.3 %shard_map.56 = f32[2,4,128]{2,1,0:T(4,128)S(1)} custom-call(s32[4]{0:T(128)S(1)} %pad_add_fusion.where, s32[3,16]{1,0:T(4,128)S(1)} %bitcast.21, s32[16]{0:T(128)S(1)} %collective-permute-done.1.pcount, bf16[1024,512]{1,0:T(8,128)(2,1)S(1)} %shard_map.55.refs_0_, bf16[1024,512]{1,0:T(8,128)(2,1)S(1)} %collective-permute-done.2.refs_1_, ...), custom_call_target="tpu_custom_call" | custom-call | tf_op jit(solution)/shard_map/pallas_call | solution.py:203
  46.2 0.1 collective-permute-start.13
  46.3 1.2 %collective-permute-done.13 = f32[2,4,128]{2,1,0:T(4,128)S(1)} collective-permute-done((f32[2,4,128]{2,1,0:T(4,128)S(1)}, f32[2,4,128]{2,1,0:T(4,128)S(1)}, u32[]{:S(2)}, u32[]{:S(2)}) %collective-permute-start.13) | collective-permute-done | bytes 4128 | tf_op jit(solution)/shard_map/ppermute | solution.py:29
  47.5 1.3 %collective-permute-start.14 = (f32[4,128]{1,0:T(4,128)S(1)}, f32[4,128]{1,0:T(4,128)S(1)}, u32[]{:S(2)}, u32[]{:S(2)}) collective-permute-start(f32[4,128]{1,0:T(4,128)S(1)} %get-tuple-element.13), channel_id=1, source_target_pairs={{0,2},{1,3},{2,0},{3,1},{4,6},{5,7},{6,4},{7,5},{8,10},{9,11},{10,... | collective-permute-start | bytes 6152 | tf_op jit(solution)/shard_map/ppermute | solution.py:29
  48.8 1.7 %collective-permute-start.16 = (f32[4,128]{1,0:T(4,128)S(1)}, f32[4,128]{1,0:T(4,128)S(1)}, u32[]{:S(2)}, u32[]{:S(2)}) collective-permute-start(f32[4,128]{1,0:T(4,128)S(1)} %get-tuple-element.14), channel_id=1, source_target_pairs={{0,6},{1,7},{2,4},{3,5},{4,2},{5,3},{6,0},{7,1},{8,14},{9,15},{10,... | collective-permute-start | bytes 6152 | tf_op jit(solution)/shard_map/ppermute | solution.py:29
  50.5 0.4 collective-permute-start.15
  51.0 0.1 collective-permute-done.14
  51.1 2.2 %collective-permute-done.16 = f32[4,128]{1,0:T(4,128)S(1)} collective-permute-done((f32[4,128]{1,0:T(4,128)S(1)}, f32[4,128]{1,0:T(4,128)S(1)}, u32[]{:S(2)}, u32[]{:S(2)}) %collective-permute-start.16) | collective-permute-done | bytes 2080 | tf_op jit(solution)/shard_map/ppermute | solution.py:29
  53.3 0.8 %collective-permute-done.15 = f32[4,128]{1,0:T(4,128)S(1)} collective-permute-done((f32[4,128]{1,0:T(4,128)S(1)}, f32[4,128]{1,0:T(4,128)S(1)}, u32[]{:S(2)}, u32[]{:S(2)}) %collective-permute-start.15) | collective-permute-done | bytes 2080 | tf_op jit(solution)/shard_map/ppermute | solution.py:29
  54.1 0.6 %dynamic-slice_reduce_fusion = f32[]{:T(128)} fusion(f32[4,128]{1,0:T(4,128)S(1)} %add_add_fusion, s32[]{:T(128)S(6)} %select_n.3), kind=kLoop, calls=%fused_computation.4 | loop fusion | flops 127 | bytes 520 | tf_op jit(solution)/shard_map/reduce_sum | solution.py:222
  (3 shorter events, 0.0 us)
Async XLA Ops:
  0.0 23.2 %copy-start.4 = (s32[16]{0:T(128)S(1)}, s32[16]{0:T(128)}, u32[]{:S(2)}) copy-start(s32[16]{0:T(128)} %param.9) | copy-start | bytes 196
  0.0 39.9 %copy-start.3 = (s32[16,3]{0,1:T(4,128)S(1)}, s32[16,3]{0,1:T(4,128)}, u32[]{:S(2)}) copy-start(s32[16,3]{0,1:T(4,128)} %param.8) | copy-start | bytes 580
  0.0 12.8 %collective-permute-start = (bf16[3,512,128]{2,1,0:T(8,128)(2,1)}, bf16[3,512,128]{2,1,0:T(8,128)(2,1)S(1)}, u32[]{:S(2)}, u32[]{:S(2)}) collective-permute-start(bf16[3,512,128]{2,1,0:T(8,128)(2,1)} %bitcast.15), channel_id=1, source_target_pairs={{0,2},{1,3},{2,0},{3,1},{4,6},{5,7},{6,4},{7,5},{8,10},{9,11},{10,... | collective-permute-start | bytes 1179656 | tf_op jit(solution)/shard_map/ppermute | solution.py:29
  2.9 20.2 %collective-permute-start.8 = (bf16[3,512,128]{2,1,0:T(8,128)(2,1)}, bf16[3,512,128]{2,1,0:T(8,128)(2,1)S(1)}, u32[]{:S(2)}, u32[]{:S(2)}) collective-permute-start(bf16[3,512,128]{2,1,0:T(8,128)(2,1)} %bitcast.16), channel_id=1, source_target_pairs={{0,8},{4,12},{8,0},{12,4},{16,28},{20,24},{24,20},{28,16},{1,9},{5... | collective-permute-start | bytes 1179656 | tf_op jit(solution)/shard_map/ppermute | solution.py:29
  5.5 17.8 %collective-permute-start.6 = (bf16[3,512,128]{2,1,0:T(8,128)(2,1)}, bf16[3,512,128]{2,1,0:T(8,128)(2,1)S(1)}, u32[]{:S(2)}, u32[]{:S(2)}) collective-permute-start(bf16[3,512,128]{2,1,0:T(8,128)(2,1)} %bitcast.17), channel_id=1, source_target_pairs={{0,4},{4,0},{8,12},{12,8},{1,5},{5,1},{9,13},{13,9},{2,6},{6,2},{1... | collective-permute-start | bytes 1179656 | tf_op jit(solution)/shard_map/ppermute | solution.py:29
  7.2 1.6 %copy-start = (bf16[512,2048]{1,0:T(8,128)(2,1)S(1)}, bf16[512,2048]{1,0:T(8,128)(2,1)}, u32[]{:S(2)}) copy-start(bf16[512,2048]{1,0:T(8,128)(2,1)} %virt_ref.1) | copy-start | bytes 6291460
  8.8 4.0 %copy-start.2 = (bf16[512,1,3,128]{3,0,2,1:T(8,128)(2,1)S(1)}, bf16[512,1,3,128]{3,0,2,1:T(8,128)(2,1)}, u32[]{:S(2)}) copy-start(bf16[512,1,3,128]{3,0,2,1:T(8,128)(2,1)} %param.5) | copy-start | bytes 1179652
  8.8 31.1 %copy-start.1 = (bf16[2048,512]{1,0:T(8,128)(2,1)S(1)}, bf16[2048,512]{1,0:T(8,128)(2,1)}, u32[]{:S(2)}) copy-start(bf16[2048,512]{1,0:T(8,128)(2,1)} %refs_12_.1) | copy-start | bytes 6291460
  10.4 26.7 %collective-permute-start.3 = (bf16[1024,512]{1,0:T(8,128)(2,1)S(1)}, bf16[1024,512]{1,0:T(8,128)(2,1)S(1)}, u32[]{:S(2)}, u32[]{:S(2)}) collective-permute-start(bf16[1024,512]{1,0:T(8,128)(2,1)S(1)} %shard_map.55.refs_0_), channel_id=1, source_target_pairs={{0,2},{1,3},{2,0},{3,1},{4,6},{5,7},{6,4},{7,5},{8,10},{9,11},{10,... | collective-permute-start | bytes 3145736 | tf_op jit(solution)/shard_map/ppermute | solution.py:29
  11.0 26.1 %collective-permute-start.2 = (bf16[1024,512]{1,0:T(8,128)(2,1)S(1)}, bf16[1024,512]{1,0:T(8,128)(2,1)S(1)}, u32[]{:S(2)}, u32[]{:S(2)}) collective-permute-start(bf16[1024,512]{1,0:T(8,128)(2,1)S(1)} %shard_map.55.refs_0_), channel_id=1, source_target_pairs={{0,1},{1,0},{2,3},{3,2},{4,5},{5,4},{6,7},{7,6},{8,9},{9,8},{10,11... | collective-permute-start | bytes 3145736 | tf_op jit(solution)/shard_map/ppermute | solution.py:29
  12.8 12.2 %collective-permute-start.4 = (bf16[3,512,128]{2,1,0:T(8,128)(2,1)S(1)}, bf16[3,512,128]{2,1,0:T(8,128)(2,1)S(1)}, u32[]{:S(2)}, u32[]{:S(2)}) collective-permute-start(bf16[3,512,128]{2,1,0:T(8,128)(2,1)S(1)} %bitcast.18), channel_id=1, source_target_pairs={{0,1},{1,0},{2,3},{3,2},{4,5},{5,4},{6,7},{7,6},{8,9},{9,8},{10,11... | collective-permute-start | bytes 1179656 | tf_op jit(solution)/shard_map/ppermute | solution.py:29
  23.2 1.1 %collective-permute-start.1 = (s32[16]{0:T(128)S(1)}, s32[16]{0:T(128)S(1)}, u32[]{:S(2)}, u32[]{:S(2)}) collective-permute-start(s32[16]{0:T(128)S(1)} %copy-done.4), channel_id=1, source_target_pairs={{0,1},{1,0},{2,3},{3,2},{4,5},{5,4},{6,7},{7,6},{8,9},{9,8},{10,11... | collective-permute-start | bytes 200 | tf_op jit(solution)/shard_map/ppermute | solution.py:29
  23.4 1.7 %collective-permute-start.7 = (bf16[3,512,128]{2,1,0:T(8,128)(2,1)S(1)}, bf16[3,512,128]{2,1,0:T(8,128)(2,1)S(1)}, u32[]{:S(2)}, u32[]{:S(2)}) collective-permute-start(bf16[3,512,128]{2,1,0:T(8,128)(2,1)S(1)} %collective-permute-done.6.refs_8_.refs_14_), channel_id=1, source_target_pairs={{0,1},{1,0},{2,3},{3,2},{4,5},{5,4},{6,7},{7,6},{8,9},{9,8},{10,11... | collective-permute-start | bytes 1179656 | tf_op jit(solution)/shard_map/ppermute | solution.py:29
  24.3 11.2 %collective-permute-start.9 = (bf16[3,512,128]{2,1,0:T(8,128)(2,1)S(1)}, bf16[3,512,128]{2,1,0:T(8,128)(2,1)S(1)}, u32[]{:S(2)}, u32[]{:S(2)}) collective-permute-start(bf16[3,512,128]{2,1,0:T(8,128)(2,1)S(1)} %collective-permute-done.refs_6_), channel_id=1, source_target_pairs={{0,4},{4,0},{8,12},{12,8},{1,5},{5,1},{9,13},{13,9},{2,6},{6,2},{1... | collective-permute-start | bytes 1179656 | tf_op jit(solution)/shard_map/ppermute | solution.py:29
  25.0 10.6 %collective-permute-start.5 = (bf16[3,512,128]{2,1,0:T(8,128)(2,1)S(1)}, bf16[3,512,128]{2,1,0:T(8,128)(2,1)S(1)}, u32[]{:S(2)}, u32[]{:S(2)}) collective-permute-start(bf16[3,512,128]{2,1,0:T(8,128)(2,1)S(1)} %collective-permute-done.refs_6_), channel_id=1, source_target_pairs={{0,1},{1,0},{2,3},{3,2},{4,5},{5,4},{6,7},{7,6},{8,9},{9,8},{10,11... | collective-permute-start | bytes 1179656 | tf_op jit(solution)/shard_map/ppermute | solution.py:29
  25.1 12.1 %collective-permute-start.11 = (bf16[3,512,128]{2,1,0:T(8,128)(2,1)S(1)}, bf16[3,512,128]{2,1,0:T(8,128)(2,1)S(1)}, u32[]{:S(2)}, u32[]{:S(2)}) collective-permute-start(bf16[3,512,128]{2,1,0:T(8,128)(2,1)S(1)} %collective-permute-done.8.refs_15_), channel_id=1, source_target_pairs={{0,16},{16,0},{1,17},{17,1},{2,18},{18,2},{3,19},{19,3},{4,20},{20... | collective-permute-start | bytes 1179656 | tf_op jit(solution)/shard_map/ppermute | solution.py:29
  35.5 1.7 %collective-permute-start.10 = (bf16[3,512,128]{2,1,0:T(8,128)(2,1)S(1)}, bf16[3,512,128]{2,1,0:T(8,128)(2,1)S(1)}, u32[]{:S(2)}, u32[]{:S(2)}) collective-permute-start(bf16[3,512,128]{2,1,0:T(8,128)(2,1)S(1)} %collective-permute-done.9.refs_10_), channel_id=1, source_target_pairs={{0,1},{1,0},{2,3},{3,2},{4,5},{5,4},{6,7},{7,6},{8,9},{9,8},{10,11... | collective-permute-start | bytes 1179656 | tf_op jit(solution)/shard_map/ppermute | solution.py:29
  37.3 2.7 %collective-permute-start.12 = (bf16[1024,512]{1,0:T(8,128)(2,1)S(1)}, bf16[1024,512]{1,0:T(8,128)(2,1)S(1)}, u32[]{:S(2)}, u32[]{:S(2)}) collective-permute-start(bf16[1024,512]{1,0:T(8,128)(2,1)S(1)} %collective-permute-done.3.refs_2_), channel_id=1, source_target_pairs={{0,1},{1,0},{2,3},{3,2},{4,5},{5,4},{6,7},{7,6},{8,9},{9,8},{10,11... | collective-permute-start | bytes 3145736 | tf_op jit(solution)/shard_map/ppermute | solution.py:29
  46.2 1.2 %collective-permute-start.13 = (f32[2,4,128]{2,1,0:T(4,128)S(1)}, f32[2,4,128]{2,1,0:T(4,128)S(1)}, u32[]{:S(2)}, u32[]{:S(2)}) collective-permute-start(f32[2,4,128]{2,1,0:T(4,128)S(1)} %shard_map.56), channel_id=1, source_target_pairs={{0,1},{1,0},{2,3},{3,2},{4,5},{5,4},{6,7},{7,6},{8,9},{9,8},{10,11... | collective-permute-start | bytes 12296 | tf_op jit(solution)/shard_map/ppermute | solution.py:29
  47.5 3.6 %collective-permute-start.14 = (f32[4,128]{1,0:T(4,128)S(1)}, f32[4,128]{1,0:T(4,128)S(1)}, u32[]{:S(2)}, u32[]{:S(2)}) collective-permute-start(f32[4,128]{1,0:T(4,128)S(1)} %get-tuple-element.13), channel_id=1, source_target_pairs={{0,2},{1,3},{2,0},{3,1},{4,6},{5,7},{6,4},{7,5},{8,10},{9,11},{10,... | collective-permute-start | bytes 6152 | tf_op jit(solution)/shard_map/ppermute | solution.py:29
  48.8 4.5 %collective-permute-start.16 = (f32[4,128]{1,0:T(4,128)S(1)}, f32[4,128]{1,0:T(4,128)S(1)}, u32[]{:S(2)}, u32[]{:S(2)}) collective-permute-start(f32[4,128]{1,0:T(4,128)S(1)} %get-tuple-element.14), channel_id=1, source_target_pairs={{0,6},{1,7},{2,4},{3,5},{4,2},{5,3},{6,0},{7,1},{8,14},{9,15},{10,... | collective-permute-start | bytes 6152 | tf_op jit(solution)/shard_map/ppermute | solution.py:29
  50.5 3.6 %collective-permute-start.15 = (f32[4,128]{1,0:T(4,128)S(1)}, f32[4,128]{1,0:T(4,128)S(1)}, u32[]{:S(2)}, u32[]{:S(2)}) collective-permute-start(f32[4,128]{1,0:T(4,128)S(1)} %get-tuple-element.14), channel_id=1, source_target_pairs={{0,4},{4,0},{8,12},{12,8},{1,5},{5,1},{9,13},{13,9},{2,6},{6,2},{1... | collective-permute-start | bytes 6152 | tf_op jit(solution)/shard_map/ppermute | solution.py:29
